TPU v7x, 256 devices: a whole 4x4x8 slice. The times are simulated.
256 devices in a mesh: mesh: 32 (over x, z), harm: 8 (over y, core).
Axes of the slice: x: 4, y: 4, z: 8, core: 2. Of those that a mesh axis runs over, the one named last changes fastest.
Arguments:
- adjoint_rhs: float32 [16, 6, 2, 65536], P('harm', None, None, 'mesh'), may hold values from -20 to 20
- forward_field: float32 [16, 2, 65536], P('harm', None, 'mesh'), may hold values from -6 to 6
- stiffness: float32 [64, 64, 4096], P(None, None, 'mesh'), may hold values from -1 to 3, as said below
- mass_blocks: float32 [64, 64, 4096], P(None, None, 'mesh'), may hold values from -1 to 3, as said below
- frequency: float32 [16], P('harm'), may hold values from 0.25 to 4
- edge_mass: float32 [65536], P('mesh'), may hold values from 0.5 to 2
- connectivity: int32 [64, 4096], P(None, 'mesh'), may hold values from 0 to 3071, as said below
- send_list: int32 [32, 2, 512], P('mesh'), may hold values from -1 to 2047, as said below
- node_block: int32 [32768], P('mesh'), may hold values from 0 to 127
- node_shape: float32 [3, 64, 32768], P(None, None, 'mesh'), may hold values from -0.1875 to 0.1875
Outputs:
- adjoint: float32 [16, 6, 2, 65536], P('harm', None, None, 'mesh')
- shape_gradient: float32 [6, 3, 32768], P(None, None, ('mesh', 'harm'))
Inputs may be any that keep to these rules, and one draw needn't show every extreme that they name: `stiffness`: each block is symmetric and its diagonal exceeds the sum of magnitudes of the other entries of its row. `mass_blocks`: each block is symmetric and its diagonal exceeds the sum of magnitudes of the other entries of its row. `send_list`: row 0 of a device lists owned edges shared with the device one lower along mesh, row 1 those shared with the device one higher; valid entries come first, then -1. A list holds at most 512 valid entries, and some device's row 0 and some device's row 1 hold exactly 512. The first device's row 0 and the last device's row 1 are empty. `connectivity`: an entry below 2048 is an edge the device owns; 2048 + k is entry k of the lower neighbour's row 1; 2560 + k is entry k of the upper neighbour's row 0. Only valid entries are named.
All inputs are finite; a program needn't handle non-finite values.
Results may differ from a plain program's by a relative error of at most 0.0003.
Values sent between devices are 32-bit elements; how exact they have to be, the bound alone decides.
No kernel may reach another device: no remote copies, remote signals or barrier semaphores. Data moves between devices by JAX's collectives and lax.ppermute only.
A program may use at most 128 MiB of HBM per device.

v0:
```python
import jax
import jax.numpy as jnp
from jax import lax
from jax.sharding import PartitionSpec as P

ITERS = 3
exact_mode = lax.Precision.HIGHEST


def extended_2(cells, sides, width):
    for axis, dim in sides:
        count = lax.axis_size(axis)
        ends = count - 1
        head = lax.slice_in_dim(cells, 0, width, axis=dim)
        tail = lax.slice_in_dim(cells, cells.shape[dim] - width, cells.shape[dim], axis=dim)
        cells = jnp.concatenate(
            [
                lax.ppermute(tail, axis, [(i, (i + 1) % count) for i in range(ends)]),
                cells,
                lax.ppermute(head, axis, [((i + 1) % count, i) for i in range(ends)]),
            ],
            axis=dim,
        )
    return cells


def from_behind(shard, axis, by):
    devices = lax.axis_size(axis)
    pairs = [(i, i + by) for i in range(devices) if 0 <= i + by < devices]
    return lax.ppermute(shard, axis, pairs)


def block_product(matrices, gathered):
    return jnp.einsum("ijb,rjb->rib", matrices, gathered, precision=exact_mode)


def per_device(
    adjoint_rhs,
    forward_field,
    stiffness,
    mass_blocks,
    frequency,
    edge_mass,
    connectivity,
    send_list,
    node_block,
    node_shape,
):
    harm_local, force_count, part_count, edge_count = adjoint_rhs.shape
    slot_count = send_list.shape[2]
    row_count = harm_local * force_count * part_count
    list_rows = send_list[0]
    is_listed = list_rows >= 0
    safe_rows = jnp.maximum(list_rows, 0)
    row_weights = jnp.repeat(frequency, force_count * part_count)
    field_weights = jnp.repeat(frequency, part_count)

    def fetch_rim(values_now):
        picked = jnp.where(is_listed[None], values_now[:, safe_rows], 0.0)
        send_buffer = picked.reshape(values_now.shape[0], 2 * slot_count)
        padded = extended_2(send_buffer, (("mesh", 1),), slot_count)
        return jnp.concatenate([padded[:, :slot_count], padded[:, 3 * slot_count :]], axis=1)

    def assemble(values_now, rim_now, weights):
        extended = jnp.concatenate([values_now, rim_now], axis=1)
        gathered = extended[:, connectivity]
        return block_product(stiffness, gathered) + weights[:, None, None] * block_product(
            mass_blocks, gathered
        )

    rhs_rows = adjoint_rhs.reshape(row_count, edge_count)
    field_rows = forward_field.reshape(harm_local * part_count, edge_count)
    first_rim = fetch_rim(rhs_rows)
    solution = jnp.zeros_like(rhs_rows)
    residual = rhs_rows

    def squares(values_now):
        return lax.psum(jnp.sum(values_now * values_now), ("mesh", "harm"))

    direction = residual
    norm_now = squares(residual)
    for iteration in range(ITERS):
        rim_now = first_rim if iteration == 0 else fetch_rim(direction)
        rows_now = direction.shape[0]
        local_terms = assemble(direction, rim_now, row_weights)
        totals = jnp.zeros((rows_now, edge_count + 2 * slot_count), jnp.float32)
        totals = totals.at[:, connectivity.reshape(-1)].add(local_terms.reshape(rows_now, -1))
        owned = totals[:, :edge_count]
        from_upper = from_behind(totals[:, edge_count : edge_count + slot_count], "mesh", -1)
        from_lower = from_behind(totals[:, edge_count + slot_count :], "mesh", 1)
        owned = owned.at[:, safe_rows[1]].add(jnp.where(is_listed[1][None], from_upper, 0.0))
        owned = owned.at[:, safe_rows[0]].add(jnp.where(is_listed[0][None], from_lower, 0.0))
        applied = owned + row_weights[:, None] * edge_mass[None, :] * direction
        step_size = norm_now / lax.psum(jnp.sum(direction * applied), ("mesh", "harm"))
        solution = solution + step_size * direction
        residual = residual - step_size * applied
        norm_next = squares(residual)
        direction = residual + norm_next / norm_now * direction
        norm_now = norm_next
    final_rims = fetch_rim(jnp.concatenate([solution, field_rows], axis=0))
    solution_rim = final_rims[:row_count]
    field_rim = final_rims[row_count:]
    block_edges, block_count = connectivity.shape
    field_terms = assemble(field_rows, field_rim, field_weights).reshape(
        harm_local, part_count, block_edges, block_count
    )
    adjoint_blocks = jnp.concatenate([solution, solution_rim], axis=1)[:, connectivity]
    adjoint_blocks = adjoint_blocks.reshape(
        harm_local, force_count, part_count, block_edges, block_count
    )
    energy_term = jnp.sum(
        adjoint_blocks[:, :, 0] * field_terms[:, None, 0]
        - adjoint_blocks[:, :, 1] * field_terms[:, None, 1],
        axis=0,
    )
    at_nodes = energy_term[:, :, node_block]
    local_grad = -jnp.einsum("kjn,ojn->okn", node_shape, at_nodes, precision=exact_mode)
    summed = lax.psum(local_grad, "harm")
    share_size = local_grad.shape[2] // lax.axis_size("harm")
    gradient = lax.dynamic_slice_in_dim(summed, lax.axis_index("harm") * share_size, share_size, 2)
    return (solution.reshape(adjoint_rhs.shape), gradient)


def solution(mesh):
    return jax.shard_map(
        per_device,
        mesh=mesh,
        in_specs=(
            P("harm", None, None, "mesh"),
            P("harm", None, "mesh"),
            P(None, None, "mesh"),
            P(None, None, "mesh"),
            P("harm"),
            P("mesh"),
            P(None, "mesh"),
            P("mesh", None, None),
            P("mesh"),
            P(None, None, "mesh"),
        ),
        out_specs=(P("harm", None, None, "mesh"), P(None, None, ("mesh", "harm"))),
        check_vma=False,
    )
```

profile of v0, /device:TPU:2, one launch (start us, length us, event | category | flops | bytes accessed | tf_op | source)
XLA Modules:
  0.0 1010.0 jit_solution(11621693017519007216)
XLA Ops:
  23.4 5.8 collective-permute-start.1
  31.7 4.5 copy.190
  36.4 5.6 copy.191
  44.0 27.7 %gather_fusion.1 = f32[8192,24]{1,0:T(8,128)} fusion(f32[24,3072]{0,1:T(8,128)S(1)} %pad_maximum_fusion, s32[8192]{0:T(1024)S(1)} %fusion.70), kind=kCustom, calls=%fused_computation.1 | custom fusion | bytes 1605632 | tf_op jit(solution)/shard_map/gather | solution.py:66
  75.4 8.8 fusion.12
  84.1 7.9 add_bitcast_fusion.2
  97.0 44.7 %scatter_custom_fusion = f32[24,3072]{0,1:T(8,128)S(1)} fusion(s32[8192]{0:T(1024)S(1)} %bitcast.176, f32[8192,24]{1,0:T(8,128)} %copy.193, f32[]{:T(128)} %constant.7.clone.1), kind=kCustom, calls=%fused_computation.48 | custom fusion | flops 196608 | bytes 295424 | tf_op jit(solution)/shard_map/scatter-add | solution.py:87
  160.3 15.4 %scatter_custom_fusion.2 = f32[24,2048]{0,1:T(8,128)S(1)} fusion(f32[24,2048]{0,1:T(8,128)S(1)} %scatter_custom_fusion.1, s32[512]{0:T(512)S(1)} %bitcast.180, f32[24,512]{0,1:T(8,128)S(1)} %collective-permute-done.3, f32[]{:T(128)} %constant.7.clone.1, pred[512]{0:T(512)(128)(4,1)S(1)} %get-tuple-element.14), kind=kCustom, calls=%fused_computation.74 | custom fusion | flops 24576 | bytes 459268 | tf_op jit(solution)/shard_map/scatter-add | solution.py:92
  176.9 74.6 %all-reduce = (f32[]{:T(128)}, f32[]{:T(128)}) all-reduce(f32[]{:T(128)} %multiply_reduce_fusion.5, f32[]{:T(128)} %multiply_reduce_fusion), channel_id=1, replica_groups=mesh['mesh'=32,'harm'=8] {'mesh','harm'}, use_global_device_ids=true, to_apply=%region_1.2 | all-reduce | flops 2 | bytes 16 | tf_op jit(solution)/shard_map/psum | solution.py:78
  253.3 73.8 %psum.51 = f32[]{:T(128)} all-reduce(f32[]{:T(128)} %get-tuple-element.18), channel_id=1, replica_groups=mesh['mesh'=32,'harm'=8] {'mesh','harm'}, use_global_device_ids=true, to_apply=%region_8.9 | all-reduce | flops 1 | bytes 8 | tf_op jit(solution)/shard_map/psum | solution.py:78
  335.2 4.5 collective-permute-start.5
  341.9 27.7 %gather_fusion.3 = f32[8192,24]{1,0:T(8,128)} fusion(f32[24,3072]{0,1:T(8,128)S(1)} %copy.200, s32[8192]{0:T(1024)S(1)} %fusion.70), kind=kCustom, calls=%fused_computation.3 | custom fusion | bytes 1605632 | tf_op jit(solution)/shard_map/gather | solution.py:66
  373.3 8.5 fusion.8
  381.9 6.6 add_bitcast_fusion.1
  392.1 45.1 %scatter_custom_fusion.3 = f32[24,3072]{0,1:T(8,128)S(1)} fusion(s32[8192]{0:T(1024)} %bitcast.177, f32[8192,24]{1,0:T(8,128)} %copy.205, f32[]{:T(128)} %constant.7.clone.1), kind=kCustom, calls=%fused_computation.46 | custom fusion | flops 196608 | bytes 295424 | tf_op jit(solution)/shard_map/scatter-add | solution.py:87
  437.6 6.4 collective-permute-start.6
  459.5 73.1 %psum.52 = f32[]{:T(128)} all-reduce(f32[]{:T(128)} %multiply_reduce_fusion.3), channel_id=1, replica_groups=mesh['mesh'=32,'harm'=8] {'mesh','harm'}, use_global_device_ids=true, to_apply=%region_13.14 | all-reduce | flops 1 | bytes 8 | tf_op jit(solution)/shard_map/psum | solution.py:94
  534.5 73.3 %psum.53 = f32[]{:T(128)} all-reduce(f32[]{:T(128)} %multiply_reduce_fusion.2), channel_id=1, replica_groups=mesh['mesh'=32,'harm'=8] {'mesh','harm'}, use_global_device_ids=true, to_apply=%region_15.16 | all-reduce | flops 1 | bytes 8 | tf_op jit(solution)/shard_map/psum | solution.py:78
  623.1 27.9 %gather_fusion.5 = f32[8192,24]{1,0:T(8,128)} fusion(f32[24,3072]{0,1:T(8,128)S(1)} %copy.212, s32[8192]{0:T(1024)S(1)} %copy-done.9), kind=kCustom, calls=%fused_computation.5 | custom fusion | bytes 1605632 | tf_op jit(solution)/shard_map/gather | solution.py:66
  654.6 8.5 fusion.4
  663.2 7.9 add_bitcast_fusion
  676.0 44.9 %scatter_custom_fusion.6 = f32[24,3072]{0,1:T(8,128)S(1)} fusion(s32[8192]{0:T(1024)} %bitcast.178, f32[8192,24]{1,0:T(8,128)} %copy.217, f32[]{:T(128)} %constant.7.clone.1), kind=kCustom, calls=%fused_computation.44 | custom fusion | flops 196608 | bytes 295424 | tf_op jit(solution)/shard_map/scatter-add | solution.py:87
  722.0 6.1 collective-permute-start.10
  743.7 73.3 %psum.54 = f32[]{:T(128)} all-reduce(f32[]{:T(128)} %multiply_reduce_fusion.1), channel_id=1, replica_groups=mesh['mesh'=32,'harm'=8] {'mesh','harm'}, use_global_device_ids=true, to_apply=%region_20.21 | all-reduce | flops 1 | bytes 8 | tf_op jit(solution)/shard_map/psum | solution.py:94
  825.8 5.9 collective-permute-start.13
  834.2 28.0 %gather_fusion.8 = f32[8192,4]{1,0:T(8,128)} fusion(f32[4,3072]{0,1:T(8,128)S(1)} %copy.225, s32[8192]{0:T(1024)S(1)} %copy-done.9), kind=kCustom, calls=%fused_computation.8 | custom fusion | bytes 294912 | tf_op jit(solution)/shard_map/gather | solution.py:66
  865.9 8.5 fusion.33
  874.4 6.6 fusion.22
  881.9 27.7 %gather_fusion.7 = f32[8192,24]{1,0:T(8,128)} fusion(f32[24,3072]{0,1:T(8,128)S(1)} %copy.223, s32[8192]{0:T(1024)S(1)} %copy-done.9), kind=kCustom, calls=%fused_computation.7 | custom fusion | bytes 1605632 | tf_op jit(solution)/shard_map/gather | solution.py:107
  913.2 9.1 gather_fusion.9
  922.3 10.0 negate_bitcast_fusion
  933.2 67.8 %all-reduce.3.cloned.1.call-done = f32[6,3,1024]{0,1,2:T(4,128)} async-done(((f32[6,3,1024]{0,1,2:T(4,128)}), f32[6,3,1024]{0,1,2:T(4,128)}) %all-reduce.3.cloned.1.call-update) | async-done | bytes 73744 | tf_op jit(solution)/shard_map/psum | solution.py:118
  (194 shorter events, 142.1 us)
Async XLA Ops:
  7.2 993.8 %all-reduce.3.cloned.1.call-start = ((), (), s32[]{:S(2)}) async-start(), calls=%async_computation | async-start | bytes 4194304 | tf_op jit(solution)/shard_map/psum | solution.py:118
  9.7 19.6 %copy-start.10 = (f32[2,6,2,2048]{3,2,1,0:T(2,128)S(1)}, f32[2,6,2,2048]{3,2,1,0:T(2,128)}, u32[]{:S(2)}) copy-start(f32[2,6,2,2048]{3,2,1,0:T(2,128)} %param.10) | copy-start | bytes 589828
  9.7 22.0 %copy-start.7 = (f32[64,64,128]{2,1,0:T(8,128)S(1)}, f32[64,64,128]{2,1,0:T(8,128)}, u32[]{:S(2)}) copy-start(f32[64,64,128]{2,1,0:T(8,128)} %param.12) | copy-start | bytes 6291460
  19.6 22.4 %collective-permute-start = (f32[24,512]{1,0:T(8,128)}, f32[24,512]{1,0:T(8,128)}, u32[]{:S(2)}, u32[]{:S(2)}) collective-permute-start(f32[24,512]{1,0:T(8,128)} %get-tuple-element.34), channel_id=1, source_target_pairs={{0,8},{8,16},{16,24},{24,32},{32,40},{40,48},{48,56},{56,64},{64,7... | collective-permute-start | bytes 147464 | tf_op jit(solution)/shard_map/ppermute | solution.py:18
  23.4 19.5 %collective-permute-start.1 = (f32[24,512]{1,0:T(8,128)}, f32[24,512]{1,0:T(8,128)}, u32[]{:S(2)}, u32[]{:S(2)}) collective-permute-start(f32[24,512]{1,0:T(8,128)} %get-tuple-element.35), channel_id=1, source_target_pairs={{8,0},{16,8},{24,16},{32,24},{40,32},{48,40},{56,48},{64,56},{72,6... | collective-permute-start | bytes 147464 | tf_op jit(solution)/shard_map/ppermute | solution.py:20
  30.8 311.1 %copy-start.8 = (s32[8192]{0:T(1024)}, s32[8192]{0:T(1024)S(1)}, u32[]{:S(2)}) copy-start(s32[8192]{0:T(1024)S(1)} %fusion.70) | copy-start | bytes 98308
  31.6 65.4 %copy-start.14 = (s32[8192,1]{0,1:T(1,128)}, s32[8192,1]{0,1:T(1,128)S(1)}, u32[]{:S(2)}) copy-start(s32[8192,1]{0,1:T(1,128)S(1)} %compare_select_fusion) | copy-start | bytes 98308
  31.6 123.3 %copy-start.27 = (s32[512,1]{0,1:T(1,128)}, s32[512,1]{0,1:T(1,128)S(1)}, u32[]{:S(2)}) copy-start(s32[512,1]{0,1:T(1,128)S(1)} %get-tuple-element.37) | copy-start | bytes 6148
  31.7 128.6 %copy-start.26 = (s32[512,1]{0,1:T(1,128)}, s32[512,1]{0,1:T(1,128)S(1)}, u32[]{:S(2)}) copy-start(s32[512,1]{0,1:T(1,128)S(1)} %get-tuple-element.36) | copy-start | bytes 6148
  31.7 123.3 %copy-start.22 = (pred[512]{0:T(512)(128)(4,1)}, pred[512]{0:T(512)(128)(4,1)S(1)}, u32[]{:S(2)}) copy-start(pred[512]{0:T(512)(128)(4,1)S(1)} %get-tuple-element.15) | copy-start | bytes 1540
  31.7 128.5 %copy-start.19 = (pred[512]{0:T(512)(128)(4,1)}, pred[512]{0:T(512)(128)(4,1)S(1)}, u32[]{:S(2)}) copy-start(pred[512]{0:T(512)(128)(4,1)S(1)} %get-tuple-element.14) | copy-start | bytes 1540
  36.4 114.6 %copy-start.15 = (f32[24]{0:T(128)}, f32[24]{0:T(128)S(1)}, u32[]{:S(2)}) copy-start(f32[24]{0:T(128)S(1)} %mul.153) | copy-start | bytes 292
  145.1 9.9 collective-permute-start.2
  149.0 11.2 %collective-permute-start.3 = (f32[24,512]{0,1:T(8,128)S(1)}, f32[24,512]{0,1:T(8,128)S(1)}, u32[]{:S(2)}, u32[]{:S(2)}) collective-permute-start(f32[24,512]{0,1:T(8,128)S(1)} %get-tuple-element.24), channel_id=1, source_target_pairs={{0,8},{8,16},{16,24},{24,32},{32,40},{40,48},{48,56},{56,64},{64,7... | collective-permute-start | bytes 147464 | tf_op jit(solution)/shard_map/ppermute | solution.py:30
  253.3 75.0 %copy-start.5 = (f32[24,2048]{1,0:T(8,128)}, f32[24,2048]{1,0:T(8,128)S(1)}, u32[]{:S(2)}) copy-start(f32[24,2048]{1,0:T(8,128)S(1)} %get-tuple-element.19) | copy-start | bytes 589828
  331.7 8.1 collective-permute-start.4
  335.2 6.2 collective-permute-start.5
  437.3 10.8 %copy-start.23 = (pred[512]{0:T(512)(128)(4,1)S(1)}, pred[512]{0:T(512)(128)(4,1)}, u32[]{:S(2)}) copy-start(pred[512]{0:T(512)(128)(4,1)} %copy-done.22) | copy-start | bytes 1540
  437.6 10.5 %collective-permute-start.6 = (f32[24,512]{0,1:T(8,128)S(1)}, f32[24,512]{0,1:T(8,128)S(1)}, u32[]{:S(2)}, u32[]{:S(2)}) collective-permute-start(f32[24,512]{0,1:T(8,128)S(1)} %get-tuple-element.23), channel_id=1, source_target_pairs={{8,0},{16,8},{24,16},{32,24},{40,32},{48,40},{56,48},{64,56},{72,6... | collective-permute-start | bytes 147464 | tf_op jit(solution)/shard_map/ppermute | solution.py:30
  444.0 10.4 %copy-start.20 = (pred[512]{0:T(512)(128)(4,1)S(1)}, pred[512]{0:T(512)(128)(4,1)}, u32[]{:S(2)}) copy-start(pred[512]{0:T(512)(128)(4,1)} %copy-done.19) | copy-start | bytes 1540
  444.0 10.4 %collective-permute-start.7 = (f32[24,512]{0,1:T(8,128)S(1)}, f32[24,512]{0,1:T(8,128)S(1)}, u32[]{:S(2)}, u32[]{:S(2)}) collective-permute-start(f32[24,512]{0,1:T(8,128)S(1)} %get-tuple-element.22), channel_id=1, source_target_pairs={{0,8},{8,16},{16,24},{24,32},{32,40},{40,48},{48,56},{56,64},{64,7... | collective-permute-start | bytes 147464 | tf_op jit(solution)/shard_map/ppermute | solution.py:30
  452.1 81.8 %copy-start.6 = (f32[24,2048]{1,0:T(8,128)S(1)}, f32[24,2048]{1,0:T(8,128)}, u32[]{:S(2)}) copy-start(f32[24,2048]{1,0:T(8,128)} %copy-done.5) | copy-start | bytes 589828
  612.5 10.5 %copy-start.9 = (s32[8192]{0:T(1024)S(1)}, s32[8192]{0:T(1024)}, u32[]{:S(2)}) copy-start(s32[8192]{0:T(1024)} %copy-done.8) | copy-start | bytes 98308
  612.6 8.1 collective-permute-start.8
  616.6 6.0 collective-permute-start.9
  721.7 10.9 %copy-start.24 = (pred[512]{0:T(512)(128)(4,1)S(1)}, pred[512]{0:T(512)(128)(4,1)}, u32[]{:S(2)}) copy-start(pred[512]{0:T(512)(128)(4,1)} %copy-done.22) | copy-start | bytes 1540
  722.0 10.5 %collective-permute-start.10 = (f32[24,512]{0,1:T(8,128)}, f32[24,512]{0,1:T(8,128)S(1)}, u32[]{:S(2)}, u32[]{:S(2)}) collective-permute-start(f32[24,512]{0,1:T(8,128)} %get-tuple-element.21), channel_id=1, source_target_pairs={{8,0},{16,8},{24,16},{32,24},{40,32},{48,40},{56,48},{64,56},{72,6... | collective-permute-start | bytes 147464 | tf_op jit(solution)/shard_map/ppermute | solution.py:30
  728.2 10.4 %copy-start.21 = (pred[512]{0:T(512)(128)(4,1)S(1)}, pred[512]{0:T(512)(128)(4,1)}, u32[]{:S(2)}) copy-start(pred[512]{0:T(512)(128)(4,1)} %copy-done.19) | copy-start | bytes 1540
  728.2 10.4 %collective-permute-start.11 = (f32[24,512]{0,1:T(8,128)S(1)}, f32[24,512]{0,1:T(8,128)S(1)}, u32[]{:S(2)}, u32[]{:S(2)}) collective-permute-start(f32[24,512]{0,1:T(8,128)S(1)} %get-tuple-element.20), channel_id=1, source_target_pairs={{0,8},{8,16},{16,24},{24,32},{32,40},{40,48},{48,56},{56,64},{64,7... | collective-permute-start | bytes 147464 | tf_op jit(solution)/shard_map/ppermute | solution.py:30
  821.8 9.9 collective-permute-start.12
  825.8 7.8 collective-permute-start.13
  913.2 9.1 copy-start.4
  (13 other events, 85.8 us)
Sparse Core Ops, SparseCore 0:
  932.5 68.3 all-reduce.2
where the time goes:
time: 1020 us; the launch traced here: 1010 us
  blocking collectives  368 us (36%)
  local copies, waits for them, and re-layouts  225 us (22%)
  other arithmetic  180 us (18%)
  waiting for transfers between devices  85.9 us (8%)
  matrix products  73.3 us (7%)
  starting transfers between devices  55.7 us (5%)
  between operations  21.8 us (2%)
    psum x3, blocking collectives, squares(): return lax.psum(jnp.sum(values_now * values_now), ('mesh', 'harm'))  222 us
    psum x2, blocking collectives, per_device(): lax.psum(jnp.sum(direction * applied), ('mesh', 'harm'))  146 us
    scatter-add x3, other arithmetic, per_device(): totals.at[:, connectivity.reshape(-1)]  135 us
    gather x8, local copies, waits for them, and re-layouts, assemble(): gathered = extended[:, connectivity]  126 us
    psum x1, waiting for transfers between devices, per_device(): summed = lax.psum(local_grad, 'harm')  67.8 us
    dot_general x8, matrix products, block_product(): return jnp.einsum('ijb,rjb->rib', matrices, gathered, precision=exact_mode)  63.2 us
    gather x2, local copies, waits for them, and re-layouts, per_device(): jnp.concatenate([solution, solution_rim], axis=1)[:, connectivity]  30.6 us
    scatter-add x3, other arithmetic, per_device(): owned.at[:, safe_rows[0]]  23.8 us
  transfers between devices with their start and end apart: 15, of which 12 were waited for; matrix products, arithmetic and copies ran while one was open for 3% of the time, Pallas kernels for 0%

commit v1 on v0

--- a/solution.py
+++ b/solution.py
@@ -115,7 +115,7 @@
     )
     at_nodes = energy_term[:, :, node_block]
     local_grad = -jnp.einsum("kjn,ojn->okn", node_shape, at_nodes, precision=exact_mode)
-    summed = lax.psum(local_grad, "harm")
+    summed = jnp.sum(lax.all_gather(local_grad, "harm"), axis=0)
     share_size = local_grad.shape[2] // lax.axis_size("harm")
     gradient = lax.dynamic_slice_in_dim(summed, lax.axis_index("harm") * share_size, share_size, 2)
     return (solution.reshape(adjoint_rhs.shape), gradient)

time: 1020 us -> 942 us (0.924)
  waiting for transfers between devices: 85.9 us -> 18.1 us
  blocking collectives: 368 us -> 382 us
  between operations: 21.8 us -> 8.43 us
  other arithmetic: 180 us -> 169 us
    psum x1 -> x0, waiting for transfers between devices: 67.8 us -> none  [per_device(): summed = lax.psum(local_grad, 'harm')]
    all_gather x0 -> x1, blocking collectives: none -> 13.5 us  [per_device(): summed = jnp.sum(lax.all_gather(local_grad, 'harm'), axis=0)]
    scatter-add x3, other arithmetic: 23.8 us -> 12.7 us  [per_device(): owned.at[:, safe_rows[0]]]
  transfers between devices with their start and end apart: 15 -> 14, of which waited for: 12 -> 11; matrix products, arithmetic and copies ran while one was open for 3% -> 3% of each run, Pallas kernels for 0% -> 0%
where the time goes in v1:
time: 942 us; the launch traced here: 932 us
  blocking collectives  382 us (41%)
  local copies, waits for them, and re-layouts  226 us (24%)
  other arithmetic  169 us (18%)
  matrix products  73.5 us (8%)
  starting transfers between devices  55.6 us (6%)
  waiting for transfers between devices  18.1 us (2%)
    psum x3, blocking collectives, squares(): return lax.psum(jnp.sum(values_now * values_now), ('mesh', 'harm'))  222 us
    psum x2, blocking collectives, per_device(): lax.psum(jnp.sum(direction * applied), ('mesh', 'harm'))  146 us
    scatter-add x3, other arithmetic, per_device(): totals.at[:, connectivity.reshape(-1)]  135 us
    gather x8, local copies, waits for them, and re-layouts, assemble(): gathered = extended[:, connectivity]  126 us
    dot_general x8, matrix products, block_product(): return jnp.einsum('ijb,rjb->rib', matrices, gathered, precision=exact_mode)  63.5 us
    gather x2, local copies, waits for them, and re-layouts, per_device(): jnp.concatenate([solution, solution_rim], axis=1)[:, connectivity]  30.6 us
    ppermute x6, starting transfers between devices, from_behind(): return lax.ppermute(shard, axis, pairs)  22.1 us
    ppermute x4, starting transfers between devices, extended_2(): lax.ppermute(head, axis, [((i + 1) % count, i) for i in range(ends)])  20.2 us
  transfers between devices with their start and end apart: 14, of which 11 were waited for; matrix products, arithmetic and copies ran while one was open for 3% of the time, Pallas kernels for 0%

profile of v1, /device:TPU:2, one launch (start us, length us, event | category | flops | bytes accessed | tf_op | source)
XLA Modules:
  0.0 932.3 jit_solution(9627047979161966027)
XLA Ops:
  16.8 5.8 collective-permute-start.1
  25.2 4.5 copy.195
  29.8 5.6 copy.196
  37.4 27.7 %gather_fusion.1 = f32[8192,24]{1,0:T(8,128)} fusion(f32[24,3072]{0,1:T(8,128)S(1)} %pad_maximum_fusion, s32[8192]{0:T(1024)S(1)} %fusion.70), kind=kCustom, calls=%fused_computation.1 | custom fusion | bytes 1605632 | tf_op jit(solution)/shard_map/gather | solution.py:66
  68.8 9.0 fusion.12
  77.8 7.9 add_bitcast_fusion.2
  90.7 44.7 %scatter_custom_fusion = f32[24,3072]{0,1:T(8,128)S(1)} fusion(s32[8192]{0:T(1024)S(1)} %bitcast.178, f32[8192,24]{1,0:T(8,128)} %copy.198, f32[]{:T(128)} %constant.7.clone.1), kind=kCustom, calls=%fused_computation.48 | custom fusion | flops 196608 | bytes 295424 | tf_op jit(solution)/shard_map/scatter-add | solution.py:87
  153.9 4.3 scatter_custom_fusion.2
  159.4 74.6 %all-reduce = (f32[]{:T(128)}, f32[]{:T(128)}) all-reduce(f32[]{:T(128)} %multiply_reduce_fusion.5, f32[]{:T(128)} %multiply_reduce_fusion), channel_id=1, replica_groups=mesh['mesh'=32,'harm'=8] {'mesh','harm'}, use_global_device_ids=true, to_apply=%region_1.2 | all-reduce | flops 2 | bytes 16 | tf_op jit(solution)/shard_map/psum | solution.py:78
  235.8 73.8 %psum.44 = f32[]{:T(128)} all-reduce(f32[]{:T(128)} %get-tuple-element.16), channel_id=1, replica_groups=mesh['mesh'=32,'harm'=8] {'mesh','harm'}, use_global_device_ids=true, to_apply=%region_8.9 | all-reduce | flops 1 | bytes 8 | tf_op jit(solution)/shard_map/psum | solution.py:78
  317.7 4.5 collective-permute-start.5
  324.4 27.7 %gather_fusion.3 = f32[8192,24]{1,0:T(8,128)} fusion(f32[24,3072]{0,1:T(8,128)S(1)} %copy.205, s32[8192]{0:T(1024)S(1)} %fusion.70), kind=kCustom, calls=%fused_computation.3 | custom fusion | bytes 1605632 | tf_op jit(solution)/shard_map/gather | solution.py:66
  355.8 8.5 fusion.8
  364.4 6.6 add_bitcast_fusion.1
  374.6 45.1 %scatter_custom_fusion.3 = f32[24,3072]{0,1:T(8,128)S(1)} fusion(s32[8192]{0:T(1024)} %bitcast.179, f32[8192,24]{1,0:T(8,128)} %copy.210, f32[]{:T(128)} %constant.7.clone.1), kind=kCustom, calls=%fused_computation.46 | custom fusion | flops 196608 | bytes 295424 | tf_op jit(solution)/shard_map/scatter-add | solution.py:87
  420.1 6.4 collective-permute-start.6
  442.0 73.1 %psum.45 = f32[]{:T(128)} all-reduce(f32[]{:T(128)} %multiply_reduce_fusion.3), channel_id=1, replica_groups=mesh['mesh'=32,'harm'=8] {'mesh','harm'}, use_global_device_ids=true, to_apply=%region_13.14 | all-reduce | flops 1 | bytes 8 | tf_op jit(solution)/shard_map/psum | solution.py:94
  517.0 73.3 %psum.46 = f32[]{:T(128)} all-reduce(f32[]{:T(128)} %multiply_reduce_fusion.2), channel_id=1, replica_groups=mesh['mesh'=32,'harm'=8] {'mesh','harm'}, use_global_device_ids=true, to_apply=%region_15.16 | all-reduce | flops 1 | bytes 8 | tf_op jit(solution)/shard_map/psum | solution.py:78
  605.6 27.9 %gather_fusion.5 = f32[8192,24]{1,0:T(8,128)} fusion(f32[24,3072]{0,1:T(8,128)S(1)} %copy.217, s32[8192]{0:T(1024)S(1)} %copy-done.9), kind=kCustom, calls=%fused_computation.5 | custom fusion | bytes 1605632 | tf_op jit(solution)/shard_map/gather | solution.py:66
  637.1 8.5 fusion.4
  645.7 7.9 add_bitcast_fusion
  658.5 44.9 %scatter_custom_fusion.6 = f32[24,3072]{0,1:T(8,128)S(1)} fusion(s32[8192]{0:T(1024)} %bitcast.180, f32[8192,24]{1,0:T(8,128)} %copy.222, f32[]{:T(128)} %constant.7.clone.1), kind=kCustom, calls=%fused_computation.44 | custom fusion | flops 196608 | bytes 295424 | tf_op jit(solution)/shard_map/scatter-add | solution.py:87
  704.6 6.1 collective-permute-start.10
  726.2 73.3 %psum.47 = f32[]{:T(128)} all-reduce(f32[]{:T(128)} %multiply_reduce_fusion.1), channel_id=1, replica_groups=mesh['mesh'=32,'harm'=8] {'mesh','harm'}, use_global_device_ids=true, to_apply=%region_20.21 | all-reduce | flops 1 | bytes 8 | tf_op jit(solution)/shard_map/psum | solution.py:94
  809.1 5.9 collective-permute-start.13
  817.5 28.0 %gather_fusion.8 = f32[8192,4]{1,0:T(8,128)} fusion(f32[4,3072]{0,1:T(8,128)S(1)} %copy.230, s32[8192]{0:T(1024)S(1)} %copy-done.9), kind=kCustom, calls=%fused_computation.8 | custom fusion | bytes 294912 | tf_op jit(solution)/shard_map/gather | solution.py:66
  849.2 8.5 fusion.33
  857.7 6.6 fusion.22
  865.2 27.7 %gather_fusion.7 = f32[8192,24]{1,0:T(8,128)} fusion(f32[24,3072]{0,1:T(8,128)S(1)} %copy.228, s32[8192]{0:T(1024)S(1)} %copy-done.9), kind=kCustom, calls=%fused_computation.7 | custom fusion | bytes 1605632 | tf_op jit(solution)/shard_map/gather | solution.py:107
  896.5 9.1 gather_fusion.9
  905.6 10.0 %negate_bitcast_fusion = f32[6,3,1024]{0,1,2:T(4,128)} fusion(f32[3,64,1024]{1,0,2:T(4,128)S(1)} %copy-done.4, f32[1024,6,64]{2,1,0:T(8,128)} %gather_fusion.9), kind=kOutput, calls=%fused_computation.21 | convolution fusion | flops 14174208 | bytes 2433024 | tf_op jit(solution)/shard_map/kjn,ojn->okn/dot_general | solution.py:117
  917.6 13.5 %all-gather = f32[48,3,1024]{2,1,0:T(4,128)S(1)} all-gather(f32[6,3,1024]{2,1,0:T(4,128)S(1)} %copy.238), channel_id=2, replica_groups=mesh['mesh'=32,'harm'=8] {'harm'}, dimensions={0}, use_global_device_ids=true | all-gather | bytes 663552 | tf_op jit(solution)/shard_map/all_gather | solution.py:118
  (193 shorter events, 143.0 us)
Async XLA Ops:
  3.1 19.6 %copy-start.10 = (f32[2,6,2,2048]{3,2,1,0:T(2,128)S(1)}, f32[2,6,2,2048]{3,2,1,0:T(2,128)}, u32[]{:S(2)}) copy-start(f32[2,6,2,2048]{3,2,1,0:T(2,128)} %param.10) | copy-start | bytes 589828
  3.1 22.0 %copy-start.7 = (f32[64,64,128]{2,1,0:T(8,128)S(1)}, f32[64,64,128]{2,1,0:T(8,128)}, u32[]{:S(2)}) copy-start(f32[64,64,128]{2,1,0:T(8,128)} %param.12) | copy-start | bytes 6291460
  13.0 22.4 %collective-permute-start = (f32[24,512]{1,0:T(8,128)}, f32[24,512]{1,0:T(8,128)}, u32[]{:S(2)}, u32[]{:S(2)}) collective-permute-start(f32[24,512]{1,0:T(8,128)} %get-tuple-element.32), channel_id=1, source_target_pairs={{0,8},{8,16},{16,24},{24,32},{32,40},{40,48},{48,56},{56,64},{64,7... | collective-permute-start | bytes 147464 | tf_op jit(solution)/shard_map/ppermute | solution.py:18
  16.8 19.5 %collective-permute-start.1 = (f32[24,512]{1,0:T(8,128)}, f32[24,512]{1,0:T(8,128)}, u32[]{:S(2)}, u32[]{:S(2)}) collective-permute-start(f32[24,512]{1,0:T(8,128)} %get-tuple-element.33), channel_id=1, source_target_pairs={{8,0},{16,8},{24,16},{32,24},{40,32},{48,40},{56,48},{64,56},{72,6... | collective-permute-start | bytes 147464 | tf_op jit(solution)/shard_map/ppermute | solution.py:20
  24.2 300.2 %copy-start.8 = (s32[8192]{0:T(1024)}, s32[8192]{0:T(1024)S(1)}, u32[]{:S(2)}) copy-start(s32[8192]{0:T(1024)S(1)} %fusion.70) | copy-start | bytes 98308
  25.0 65.6 %copy-start.14 = (s32[8192,1]{0,1:T(1,128)}, s32[8192,1]{0,1:T(1,128)S(1)}, u32[]{:S(2)}) copy-start(s32[8192,1]{0,1:T(1,128)S(1)} %compare_select_fusion) | copy-start | bytes 98308
  25.1 123.6 %copy-start.27 = (s32[512,1]{0,1:T(1,128)}, s32[512,1]{0,1:T(1,128)S(1)}, u32[]{:S(2)}) copy-start(s32[512,1]{0,1:T(1,128)S(1)} %get-tuple-element.35) | copy-start | bytes 6148
  25.1 128.9 %copy-start.26 = (s32[512,1]{0,1:T(1,128)}, s32[512,1]{0,1:T(1,128)S(1)}, u32[]{:S(2)}) copy-start(s32[512,1]{0,1:T(1,128)S(1)} %get-tuple-element.34) | copy-start | bytes 6148
  25.1 123.5 %copy-start.22 = (pred[512]{0:T(512)(128)(4,1)}, pred[512]{0:T(512)(128)(4,1)S(1)}, u32[]{:S(2)}) copy-start(pred[512]{0:T(512)(128)(4,1)S(1)} %get-tuple-element.13) | copy-start | bytes 1540
  25.1 128.8 %copy-start.19 = (pred[512]{0:T(512)(128)(4,1)}, pred[512]{0:T(512)(128)(4,1)S(1)}, u32[]{:S(2)}) copy-start(pred[512]{0:T(512)(128)(4,1)S(1)} %get-tuple-element.12) | copy-start | bytes 1540
  29.8 114.8 %copy-start.15 = (f32[24]{0:T(128)}, f32[24]{0:T(128)S(1)}, u32[]{:S(2)}) copy-start(f32[24]{0:T(128)S(1)} %mul.153) | copy-start | bytes 292
  68.8 9.1 copy-start
  138.8 9.9 %collective-permute-start.2 = (f32[24,512]{0,1:T(8,128)}, f32[24,512]{0,1:T(8,128)S(1)}, u32[]{:S(2)}, u32[]{:S(2)}) collective-permute-start(f32[24,512]{0,1:T(8,128)} %get-tuple-element.23), channel_id=1, source_target_pairs={{8,0},{16,8},{24,16},{32,24},{40,32},{48,40},{56,48},{64,56},{72,6... | collective-permute-start | bytes 147464 | tf_op jit(solution)/shard_map/ppermute | solution.py:30
  142.7 11.2 %collective-permute-start.3 = (f32[24,512]{0,1:T(8,128)S(1)}, f32[24,512]{0,1:T(8,128)S(1)}, u32[]{:S(2)}, u32[]{:S(2)}) collective-permute-start(f32[24,512]{0,1:T(8,128)S(1)} %get-tuple-element.22), channel_id=1, source_target_pairs={{0,8},{8,16},{16,24},{24,32},{32,40},{40,48},{48,56},{56,64},{64,7... | collective-permute-start | bytes 147464 | tf_op jit(solution)/shard_map/ppermute | solution.py:30
  235.8 75.0 %copy-start.5 = (f32[24,2048]{1,0:T(8,128)}, f32[24,2048]{1,0:T(8,128)S(1)}, u32[]{:S(2)}) copy-start(f32[24,2048]{1,0:T(8,128)S(1)} %get-tuple-element.17) | copy-start | bytes 589828
  314.2 8.1 collective-permute-start.4
  317.7 6.2 collective-permute-start.5
  419.8 10.8 %copy-start.23 = (pred[512]{0:T(512)(128)(4,1)S(1)}, pred[512]{0:T(512)(128)(4,1)}, u32[]{:S(2)}) copy-start(pred[512]{0:T(512)(128)(4,1)} %copy-done.22) | copy-start | bytes 1540
  420.1 10.5 %collective-permute-start.6 = (f32[24,512]{0,1:T(8,128)S(1)}, f32[24,512]{0,1:T(8,128)S(1)}, u32[]{:S(2)}, u32[]{:S(2)}) collective-permute-start(f32[24,512]{0,1:T(8,128)S(1)} %get-tuple-element.21), channel_id=1, source_target_pairs={{8,0},{16,8},{24,16},{32,24},{40,32},{48,40},{56,48},{64,56},{72,6... | collective-permute-start | bytes 147464 | tf_op jit(solution)/shard_map/ppermute | solution.py:30
  426.5 10.4 %copy-start.20 = (pred[512]{0:T(512)(128)(4,1)S(1)}, pred[512]{0:T(512)(128)(4,1)}, u32[]{:S(2)}) copy-start(pred[512]{0:T(512)(128)(4,1)} %copy-done.19) | copy-start | bytes 1540
  426.5 10.4 %collective-permute-start.7 = (f32[24,512]{0,1:T(8,128)S(1)}, f32[24,512]{0,1:T(8,128)S(1)}, u32[]{:S(2)}, u32[]{:S(2)}) collective-permute-start(f32[24,512]{0,1:T(8,128)S(1)} %get-tuple-element.20), channel_id=1, source_target_pairs={{0,8},{8,16},{16,24},{24,32},{32,40},{40,48},{48,56},{56,64},{64,7... | collective-permute-start | bytes 147464 | tf_op jit(solution)/shard_map/ppermute | solution.py:30
  434.6 81.8 %copy-start.6 = (f32[24,2048]{1,0:T(8,128)S(1)}, f32[24,2048]{1,0:T(8,128)}, u32[]{:S(2)}) copy-start(f32[24,2048]{1,0:T(8,128)} %copy-done.5) | copy-start | bytes 589828
  595.0 10.5 %copy-start.9 = (s32[8192]{0:T(1024)S(1)}, s32[8192]{0:T(1024)}, u32[]{:S(2)}) copy-start(s32[8192]{0:T(1024)} %copy-done.8) | copy-start | bytes 98308
  595.1 8.1 collective-permute-start.8
  599.1 6.0 collective-permute-start.9
  704.3 10.9 %copy-start.24 = (pred[512]{0:T(512)(128)(4,1)S(1)}, pred[512]{0:T(512)(128)(4,1)}, u32[]{:S(2)}) copy-start(pred[512]{0:T(512)(128)(4,1)} %copy-done.22) | copy-start | bytes 1540
  704.6 10.5 %collective-permute-start.10 = (f32[24,512]{0,1:T(8,128)}, f32[24,512]{0,1:T(8,128)S(1)}, u32[]{:S(2)}, u32[]{:S(2)}) collective-permute-start(f32[24,512]{0,1:T(8,128)} %get-tuple-element.19), channel_id=1, source_target_pairs={{8,0},{16,8},{24,16},{32,24},{40,32},{48,40},{56,48},{64,56},{72,6... | collective-permute-start | bytes 147464 | tf_op jit(solution)/shard_map/ppermute | solution.py:30
  710.7 10.4 %copy-start.21 = (pred[512]{0:T(512)(128)(4,1)S(1)}, pred[512]{0:T(512)(128)(4,1)}, u32[]{:S(2)}) copy-start(pred[512]{0:T(512)(128)(4,1)} %copy-done.19) | copy-start | bytes 1540
  710.7 10.4 %collective-permute-start.11 = (f32[24,512]{0,1:T(8,128)S(1)}, f32[24,512]{0,1:T(8,128)S(1)}, u32[]{:S(2)}, u32[]{:S(2)}) collective-permute-start(f32[24,512]{0,1:T(8,128)S(1)} %get-tuple-element.18), channel_id=1, source_target_pairs={{0,8},{8,16},{16,24},{24,32},{32,40},{40,48},{48,56},{56,64},{64,7... | collective-permute-start | bytes 147464 | tf_op jit(solution)/shard_map/ppermute | solution.py:30
  804.3 10.7 %collective-permute-start.12 = (f32[28,512]{1,0:T(8,128)S(1)}, f32[28,512]{1,0:T(8,128)S(1)}, u32[]{:S(2)}, u32[]{:S(2)}) collective-permute-start(f32[28,512]{1,0:T(8,128)S(1)} %get-tuple-element.27), channel_id=1, source_target_pairs={{0,8},{8,16},{16,24},{24,32},{32,40},{40,48},{48,56},{56,64},{64,7... | collective-permute-start | bytes 172040 | tf_op jit(solution)/shard_map/ppermute | solution.py:18
  809.1 7.8 collective-permute-start.13
  896.5 9.1 copy-start.4
  (12 other events, 77.0 us)
